TPU v7x, 32 devices: a whole 2x2x4 slice. The times are simulated.
32 devices in a mesh: blk: 4 (over x, core), sub: 4 (over z), rows: 2 (over y).
Axes of the slice: x: 2, y: 2, z: 4, core: 2. Of those that a mesh axis runs over, the one named last changes fastest.
Arguments:
- bem_matrix: bfloat16 [2, 4096, 32768], P(None, ('sub', 'rows'), 'blk'), may hold values from -0.0234375 to 0.0234375
- surface_field: bfloat16 [32768, 2, 128], P(('blk', 'sub', 'rows')), may hold values from -6 to 6
- owner: int32 [4096], P(('sub', 'rows')), may hold values from 0 to 7, as said below
- wet_offset: int32 [8], replicated, may hold values from 0 to 511
- wet_count: int32 [8], replicated, may hold values from 128 to 512
- coupling: float32 [8, 512, 512], P(('sub', 'rows')), may hold values from -0.25 to 0.25
Outputs:
- forces: float32 [8, 2, 128, 512], P(('sub', 'rows'), None, 'blk')
Inputs may be any that keep to these rules, and one draw needn't show every extreme that they name: `owner`: in each aligned block of 512 rows (the rows of one index of sub and rows), no subdomain is named by more than 128 rows, and one subdomain is named by exactly 128 rows in every block.
All inputs are finite; a program needn't handle non-finite values.
Results may differ from a plain program's by a relative error of at most 0.0003.
Values may be sent and summed in bfloat16 or wider, within the bound.
A program may use at most 64 MiB of HBM per device.

v0:
```python
import jax
import jax.numpy as jnp
from jax import lax
from jax.sharding import PartitionSpec as P


def carried_in(value, axis, join, neutral):
    count, mine = (lax.axis_size(axis), lax.axis_index(axis))
    pieces = lax.all_gather(value, axis)
    running = jnp.full_like(value, 0) + jnp.asarray(neutral, value.dtype)

    def step(position, running):
        longer = join(running, pieces[position])
        return jnp.where(position < mine, longer, running)

    return lax.fori_loop(0, count - 1, step, running)


def shards(bem_matrix, surface_field, owner, wet_offset, wet_count, coupling):
    local_rows = bem_matrix.shape[1]
    local_cols = bem_matrix.shape[2]
    vectors = surface_field.shape[2]
    subdomains = wet_count.shape[0]
    wet_rows = coupling.shape[1]
    capacity = 2 * local_rows // subdomains
    stacked = bem_matrix.reshape(2 * local_rows, local_cols)
    piece = lax.all_gather(surface_field, ("sub", "rows"), axis=0, tiled=True)
    flat_piece = piece.reshape(piece.shape[0], 2 * vectors)
    products = jnp.dot(stacked, flat_piece, preferred_element_type=jnp.float32)
    products = products.reshape(2, local_rows, 2, vectors)
    real_part = products[0, :, 0] - products[1, :, 1]
    imag_part = products[1, :, 0] + products[0, :, 1]
    partial_pressure = jnp.stack([real_part, imag_part], axis=1)
    table = (owner[:, None] == jnp.arange(subdomains, dtype=jnp.int32)[None, :]).astype(jnp.int32)
    earlier_here = jnp.cumsum(table, axis=0) - table
    local_rank = jnp.sum(earlier_here * table, axis=1)
    own_counts = jnp.sum(table, axis=0)
    before = carried_in(
        own_counts,
        ("sub", "rows"),
        lambda first, second: first + second,
        jnp.zeros_like(own_counts),
    )
    rank = before[owner] + local_rank
    is_wet = rank < wet_count[owner]
    slot = (wet_offset[owner] + rank) % wet_rows
    slot_value = jnp.where(is_wet, slot, -1).astype(jnp.float32)
    row_values = partial_pressure.reshape(local_rows, -1)
    width = row_values.shape[1]
    target = owner * capacity + local_rank
    select_rows = (
        target[:, None] == jnp.arange(subdomains * capacity, dtype=jnp.int32)[None, :]
    ).astype(jnp.float32)
    contract_rows = (((0,), (0,)), ((), ()))
    sent_values = lax.dot_general(
        select_rows,
        row_values,
        contract_rows,
        precision=lax.Precision.HIGHEST,
        preferred_element_type=jnp.float32,
    ).reshape(subdomains, capacity, width)
    placed_slots = lax.dot_general(
        select_rows,
        (slot_value + 1.0)[:, None],
        contract_rows,
        precision=lax.Precision.HIGHEST,
        preferred_element_type=jnp.float32,
    )
    sent_slots = (placed_slots[:, 0] - 1.0).reshape(subdomains, capacity)
    got_values, got_slots = (
        lax.all_to_all(sent_values, ("sub", "rows"), split_axis=0, concat_axis=0, tiled=True),
        lax.all_to_all(sent_slots, ("sub", "rows"), split_axis=0, concat_axis=0, tiled=True),
    )
    spread = got_values.reshape(subdomains, capacity, 2, vectors)
    got_values = lax.psum_scatter(spread, "blk", scatter_dimension=3, tiled=True).reshape(
        subdomains, capacity, -1
    )
    final_width = got_values.shape[2]
    flat_values = got_values.reshape(subdomains * capacity, final_width)
    flat_slots = got_slots.reshape(subdomains * capacity)
    placement = (flat_slots[:, None] == jnp.arange(wet_rows, dtype=jnp.float32)[None, :]).astype(
        jnp.float32
    )
    wet_block = lax.dot_general(
        placement,
        flat_values,
        (((0,), (0,)), ((), ())),
        precision=lax.Precision.HIGHEST,
        preferred_element_type=jnp.float32,
    )
    loads = lax.dot_general(
        wet_block,
        coupling[0],
        (((0,), (0,)), ((), ())),
        precision=lax.Precision.HIGHEST,
        preferred_element_type=jnp.float32,
    )
    return loads.reshape(1, 2, final_width // 2, coupling.shape[2])


def solution(mesh):
    return jax.shard_map(
        shards,
        mesh=mesh,
        in_specs=(
            P(None, ("sub", "rows"), "blk"),
            P(("blk", "sub", "rows"), None, None),
            P(("sub", "rows")),
            P(),
            P(),
            P(("sub", "rows"), None, None),
        ),
        out_specs=P(("sub", "rows"), None, "blk", None),
        check_vma=False,
    )
```

profile of v0, /device:TPU:0, one launch (start us, length us, event | category | flops | bytes accessed | tf_op | source)
XLA Modules:
  0.0 177.1 jit_solution(7426326448940702195)
XLA Ops:
  6.5 0.0 copy-start
  6.5 0.0 all-gather.3.cloned.1.call-start
  6.5 0.7 all-gather.3.cloned.1.call-update
  7.3 0.7 fusion.18
  7.9 1.1 reduce-window.6
  9.1 0.2 slice_reduce_fusion
  9.3 0.9 convert_reduce_fusion
  10.2 0.7 multiply_add_fusion.1
  10.9 74.7 %all-gather.3.cloned.1.call-done = bf16[8192,2,128]{2,1,0:T(2,128)(2,1)} async-done(((bf16[1024,2,128]{2,1,0:T(2,128)(2,1)}), bf16[8192,2,128]{2,1,0:T(2,128)(2,1)}) %all-gather.3.cloned.1.call-update) | async-done | bytes 4194320 | tf_op jit(solution)/shard_map/all_gather | solution.py:27
  85.6 11.2 %copy.17 = bf16[8192,2,128]{0,2,1:T(8,128)(2,1)} copy(bf16[8192,2,128]{2,1,0:T(2,128)(2,1)} %all-gather.3.cloned.1.call-done) | data formatting | bytes 8388608 | tf_op jit(solution)/shard_map/reshape | solution.py:28
  96.8 9.3 %fusion = f32[2,512,2,128]{1,3,2,0:T(8,128)S(1)} fusion(bf16[2,512,8192]{2,1,0:T(8,128)(2,1)} %param.8, bf16[8192,2,128]{0,2,1:T(8,128)(2,1)} %copy.17), kind=kOutput, calls=%fused_computation.2 | convolution fusion | flops 4294967296 | bytes 22020096 | tf_op jit(solution)/shard_map/dot_general | solution.py:29
  106.2 0.0 copy-start.4
  106.2 0.0 copy-start.2
  106.2 0.0 copy-start.3
  106.2 0.1 fusion.15
  106.4 2.1 %fusion.4 = f32[8,128,256]{2,1,0:T(8,128)} fusion(f32[512,256,1]{0,1,2:T(8,128)S(1)} %bitcast.100, s32[8,128]{1,0:T(8,128)S(1)} %multiply_add_fusion, s32[512]{0:T(512)S(1)} %multiply_add_fusion.1), kind=kOutput, calls=%fused_computation.8 | convolution fusion | flops 1611137024 | bytes 1579008 | tf_op jit(solution)/shard_map/dot_general | solution.py:55
  108.4 3.6 %all-to-all-start = ((f32[8,128,256]{2,1,0:T(8,128)}), f32[8,128,256]{2,1,0:T(8,128)S(1)}, u32[]{:S(2)}, u32[]{:S(2)}) async-start(f32[8,128,256]{2,1,0:T(8,128)} %fusion.4), calls=%async_computation | async-start | bytes 2097152 | tf_op jit(solution)/shard_map/all_to_all | solution.py:71
  112.0 0.0 copy-start.1
  112.0 0.0 reduce-scatter.5.cloned.1.call-start
  112.1 0.0 copy-done.4
  112.1 0.6 dynamic-slice
  113.3 0.2 dynamic-update-slice
  113.6 24.0 %all-reduce = s32[64]{0:T(128)S(1)} all-reduce(s32[64]{0:T(128)S(1)} %dynamic-update-slice), channel_id=2, replica_groups=mesh['blk'=4,'sub'=4,'rows'=2] {'sub','rows'}, use_global_device_ids=true, to_apply=%add | all-reduce | flops 64 | bytes 512
  137.6 0.1 reshape.165
  137.7 0.0 copy-done.2
  137.7 0.7 fusion.25
  138.4 0.0 copy-done.3
  138.4 0.7 fusion.24
  139.0 0.0 all-to-all-done
  139.1 0.4 copy.19
  139.5 0.1 copy.20
  139.6 1.3 copy.27
  140.9 0.0 reduce-scatter.5.cloned.1.call-update
  140.9 0.3 while.14
  141.2 0.7 fusion.23
  141.9 0.0 copy-done.1
  141.9 14.9 %fusion.22 = f32[512]{0:T(512)S(1)} fusion(s32[512]{0:T(512)S(1)} %get-tuple-element.101, s32[512]{0:T(512)S(1)} %copy-done.1, s32[]{:T(128)} %bitcast.33, s32[]{:T(128)} %bitcast.34, s32[]{:T(128)} %bitcast.35, s32[]{:T(128)} %bitcast.36, s32[]{:T(128)} %bitcast.37, s32[]{:T(128)} %bitcast.38, s32[]{:T(128)} %bitcast.39, s32[]{:T(128)} %bitcast.40, ...), kind=kLoop, calls=%fused_computation.41 | loop fusion | flops 24576 | bytes 6240 | tf_op jit(solution)/shard_map/add | solution.py:64
  156.8 0.8 fusion.8
  157.6 0.6 broadcast_add_fusion
  158.2 3.4 %all-to-all-start.1 = ((f32[8,1,128]{2,1,0:T(1,128)}), f32[8,1,128]{2,1,0:T(1,128)S(1)}, u32[]{:S(2)}, u32[]{:S(2)}) async-start(f32[8,1,128]{2,1,0:T(1,128)} %bitcast.43), calls=%async_computation.1 | async-start | bytes 8192 | tf_op jit(solution)/shard_map/all_to_all | solution.py:72
  161.5 3.2 %reduce-scatter.5.cloned.1.call-done = f32[32,2048]{1,0:T(8,128)} async-done(((f32[128,2048]{1,0:T(8,128)}), f32[32,2048]{1,0:T(8,128)}) %reduce-scatter.5.cloned.1.call-update) | async-done | bytes 262160
  164.7 1.0 copy.23
  165.8 2.1 %all-to-all-done.1 = f32[8,1,128]{2,1,0:T(1,128)S(1)} async-done(((f32[8,1,128]{2,1,0:T(1,128)}), f32[8,1,128]{2,1,0:T(1,128)S(1)}, u32[]{:S(2)}, u32[]{:S(2)}) %all-to-all-start.1) | async-done | bytes 4128 | tf_op jit(solution)/shard_map/all_to_all | solution.py:72
  167.9 0.9 fusion.6
  168.8 0.0 copy-done
  168.8 1.4 convolution_bitcast_fusion
  (15 shorter events, 0.3 us)
Async XLA Ops:
  6.5 162.3 %copy-start = (f32[1,512,512]{2,1,0:T(8,128)S(1)}, f32[1,512,512]{2,1,0:T(8,128)}, u32[]{:S(2)}) copy-start(f32[1,512,512]{2,1,0:T(8,128)} %param.13) | copy-start | bytes 3145732
  6.5 79.1 %all-gather.3.cloned.1.call-start = ((), (), s32[]{:S(2)}) async-start(), calls=%async_computation.3 | async-start | bytes 4718592 | tf_op jit(solution)/shard_map/all_gather | solution.py:27
  106.2 5.9 %copy-start.4 = (u32[32]{0:T(128)S(1)}, u32[32]{0:T(128)}, u32[]{:S(2)}) copy-start(u32[32]{0:T(128)} %constant.93) | copy-start | bytes 388
  106.2 31.5 %copy-start.2 = (s32[8]{0:T(128)S(1)}, s32[8]{0:T(128)}, u32[]{:S(2)}) copy-start(s32[8]{0:T(128)} %param.11) | copy-start | bytes 100
  106.2 32.2 %copy-start.3 = (s32[8]{0:T(128)S(1)}, s32[8]{0:T(128)}, u32[]{:S(2)}) copy-start(s32[8]{0:T(128)} %param.12) | copy-start | bytes 100
  108.4 30.6 %all-to-all-start = ((f32[8,128,256]{2,1,0:T(8,128)}), f32[8,128,256]{2,1,0:T(8,128)S(1)}, u32[]{:S(2)}, u32[]{:S(2)}) async-start(f32[8,128,256]{2,1,0:T(8,128)} %fusion.4), calls=%async_computation | async-start | bytes 2097152 | tf_op jit(solution)/shard_map/all_to_all | solution.py:71
  112.0 29.9 %copy-start.1 = (s32[512]{0:T(512)S(1)}, s32[512]{0:T(512)}, u32[]{:S(2)}) copy-start(s32[512]{0:T(512)} %param.10) | copy-start | bytes 6148
  112.0 52.7 %reduce-scatter.5.cloned.1.call-start = ((), (), s32[]{:S(2)}) async-start(), calls=%async_computation.4 | async-start | bytes 1310720
  158.2 9.8 %all-to-all-start.1 = ((f32[8,1,128]{2,1,0:T(1,128)}), f32[8,1,128]{2,1,0:T(1,128)S(1)}, u32[]{:S(2)}, u32[]{:S(2)}) async-start(f32[8,1,128]{2,1,0:T(1,128)} %bitcast.43), calls=%async_computation.1 | async-start | bytes 8192 | tf_op jit(solution)/shard_map/all_to_all | solution.py:72
Sparse Core Ops, SparseCore 0:
  9.5 76.0 all-gather.2
  141.0 23.6 reduce-scatter.4
where the time goes:
time: 178 us; the launch traced here: 177 us
  waiting for transfers between devices  80.7 us (45%)
  blocking collectives  24 us (13%)
  other arithmetic  19.2 us (11%)
  local copies, waits for them, and re-layouts  17.3 us (10%)
  matrix products  14.5 us (8%)
  between operations  14.2 us (8%)
  starting transfers between devices  6.97 us (4%)
    all_gather x1, waiting for transfers between devices, shards(): piece = lax.all_gather(surface_field, ('sub', 'rows'), axis=0, tiled=True)  74.7 us
    unnamed x1, blocking collectives  24 us
    add x1, other arithmetic, shards(): slot_value + 1.0  14.9 us
    reshape x1, local copies, waits for them, and re-layouts, shards(): flat_piece = piece.reshape(piece.shape[0], 2 * vectors)  11.2 us
    dot_general x1, matrix products, shards(): products = jnp.dot(stacked, flat_piece, preferred_element_type=jnp.float32)  9.35 us
    unnamed x3, waiting for transfers between devices  3.93 us
  transfers between devices with their start and end apart: 4, of which 3 were waited for; matrix products, arithmetic and copies ran while one was open for 14% of the time, Pallas kernels for 0%

commit v1 on v0

v1 whole, which is shorter than its diff:
```python
import functools

import jax
import jax.numpy as jnp
from jax import lax
from jax.experimental import pallas as pl
from jax.experimental.pallas import tpu as pltpu
from jax.sharding import PartitionSpec as P

MESH = pl.DeviceIdType.MESH
BF = jnp.bfloat16
F32 = jnp.float32
HALVES = 2
NN = (((1,), (0,)), ((), ()))
NT = (((1,), (1,)), ((), ()))


def dot(a, b, dims):
    return lax.dot_general(a, b, dims, preferred_element_type=F32)


def split(x, parts):
    out = []
    for _ in range(parts):
        top = x.astype(BF)
        out.append(top)
        x = x - top.astype(F32)
    return out


def kernel(
    dims,
    a_ref, x_ref, owner_ref, off_ref, cnt_ref, coup_ref,
    out_ref,
    ab, xb, acc, rb, cb, st, gh, gl, pk, sb,
    a_sem, z_recv, e_recv, up_send, down_send, y_send, e_send,
    r_send, r_recv, c_send, c_recv, p_send, p_recv,
):
    nz, nb, vv, depth, cap = dims
    ns = 2 * nz
    rows = ab.shape[2]
    wet = coup_ref.shape[1]
    wide = xb.shape[2]
    half = wide // 2
    b, z, y = (lax.axis_index(name) for name in ("blk", "sub", "rows"))
    me = z * 2 + y
    pair = z + 1 - 2 * lax.rem(z, 2)

    barrier = pltpu.get_barrier_semaphore()
    peers = []
    for d in range(1, ns):
        other = lax.rem(me + d, ns)
        peers.append((b, other // 2, lax.rem(other, 2)))
    mates = [(lax.rem(b + d, nb), z, y) for d in range(1, nb)]
    for who in peers + mates:
        pl.semaphore_signal(barrier, inc=1, device_id=who, device_id_type=MESH)

    def a_copy(shard):
        return pltpu.make_async_copy(
            a_ref.at[:, :, pl.ds(pl.multiple_of(shard * depth, depth), depth)],
            ab.at[shard],
            a_sem.at[shard],
        )

    def near(k):
        if k == 0:
            return [(z, None)]
        return [(z - k, z - k >= 0), (z + k, z + k < nz)]

    def guarded(cond, body):
        if cond is None:
            body()
        else:
            pl.when(cond)(body)

    for k in range(nz):
        for zs, cond in near(k):

            def load(zs=zs):
                a_copy(zs * 2 + y).start()
                a_copy(zs * 2 + 1 - y).start()

            guarded(cond, load)

    pl.semaphore_wait(barrier, len(peers) + len(mates))

    def remote(src, dst, send, recv, who):
        return pltpu.make_async_remote_copy(
            src_ref=src, dst_ref=dst, send_sem=send, recv_sem=recv,
            device_id=who, device_id_type=MESH,
        )

    def up(h, zs):
        src = x_ref.at[h] if zs is z else xb.at[h, zs * 2 + y]
        return remote(src, xb.at[h, zs * 2 + y], up_send.at[h, zs], z_recv.at[h, zs * 2 + y], (b, z + 1, y))

    def down(h, zs):
        src = x_ref.at[h] if zs is z else xb.at[h, zs * 2 + y]
        return remote(src, xb.at[h, zs * 2 + y], down_send.at[h, zs], z_recv.at[h, zs * 2 + y], (b, z - 1, y))

    def across(h, zs):
        src = x_ref.at[h] if zs is z else xb.at[h, zs * 2 + y]
        return remote(src, xb.at[h, zs * 2 + y], y_send.at[h, zs], z_recv.at[h, zs * 2 + y], (b, z, 1 - y))

    def across_part(h):
        rows_ = pl.ds(0, half)
        slot = pair * 2 + y
        return remote(xb.at[h, slot, rows_], xb.at[h, slot, rows_], y_send.at[h, pair], z_recv.at[h, slot], (b, z, 1 - y))

    def extra(h):
        rows_ = pl.ds(half, half)
        slot = z * 2 + 1 - y
        return remote(xb.at[h, slot, rows_], xb.at[h, slot, rows_], e_send.at[h], e_recv.at[h], (b, pair, y))

    def arrived(h, slot):
        pltpu.make_async_copy(xb.at[h, slot], xb.at[h, slot], z_recv.at[h, slot]).wait()

    def arrived_pair(h):
        slot = pair * 2 + 1 - y
        low, high = pl.ds(0, half), pl.ds(half, half)
        pltpu.make_async_copy(xb.at[h, slot, low], xb.at[h, slot, low], z_recv.at[h, slot]).wait()
        pltpu.make_async_copy(xb.at[h, slot, high], xb.at[h, slot, high], e_recv.at[h]).wait()

    def start_own(h):
        across(h, z).start()
        pl.when(z < nz - 1)(lambda: up(h, z).start())
        pl.when(z > 0)(lambda: down(h, z).start())

    def multiply(h, shard, x, first=False):
        p = x.shape[0] // 2
        turned = jnp.concatenate([-x[p:], x[:p]], axis=0)
        total = dot(x, ab[shard, 0], NT) + dot(turned, ab[shard, 1], NT)
        total = total.reshape(2, nb, vv, rows)
        if first:
            acc[h] = total
        else:
            acc[h] += total

    start_own(0)

    owner = owner_ref[...]
    table = (lax.broadcasted_iota(jnp.int32, (ns, rows), 0) == owner).astype(F32)
    before_me = (
        lax.broadcasted_iota(jnp.int32, (rows, rows), 0)
        < lax.broadcasted_iota(jnp.int32, (rows, rows), 1)
    ).astype(F32).astype(BF)
    earlier = dot(table.astype(BF), before_me, NN)
    local_rank = jnp.sum(earlier * table, axis=0, keepdims=True).astype(jnp.int32)
    counts = jnp.sum(table, axis=1, keepdims=True)
    cb[me] = jnp.broadcast_to(counts, (ns, 128))
    count_copies = [
        remote(cb.at[me], cb.at[me], c_send.at[d], c_recv.at[d], who)
        for d, who in enumerate(peers)
    ]
    for c in count_copies:
        c.start()
    place = lax.broadcasted_iota(jnp.int32, (cap, rows), 0)
    for o in range(ns):
        st[o * cap : (o + 1) * cap] = (
            jnp.where((owner == o) & (local_rank == place), 1.0, 0.0).astype(BF)
        )

    def prepare():
        for d, c in enumerate(count_copies):
            c.wait_send()
            src = lax.rem(me + ns - 1 - d, ns)
            remote(cb.at[src], cb.at[src], c_send.at[d], c_recv.at[d], peers[d]).wait_recv()
        offset, limit = off_ref[me], cnt_ref[me]
        c_high, c_low = split(coup_ref[0], 2)
        mine = lax.broadcasted_iota(jnp.int32, (ns, 128), 0) == me
        at = lax.broadcasted_iota(jnp.int32, (cap, wet), 0)
        w = lax.broadcasted_iota(jnp.int32, (cap, wet), 1)
        before = jnp.zeros((1, wet), jnp.int32)
        for s in range(ns):
            here = jnp.sum(jnp.where(mine, cb[s], 0.0), axis=0, keepdims=True)
            here = jnp.concatenate([here] * (wet // 128), axis=1).astype(jnp.int32)
            rank = before + at
            slot = (rank + offset) & (wet - 1)
            hit = jnp.where((slot == w) & (rank < limit) & (at < here), 1.0, 0.0).astype(BF)
            gh[s * cap : (s + 1) * cap] = dot(hit, c_high, NN).astype(BF)
            gl[s * cap : (s + 1) * cap] = dot(hit, c_low, NN).astype(BF)
            before = before + here

    def reduce_copies(h):
        return [
            remote(acc.at[h, :, who[0]], rb.at[h, d], r_send.at[h, d], r_recv.at[h, d], who)
            for d, who in enumerate(mates)
        ]

    def regroup_copies(h):
        return [
            remote(pk.at[h, who[1] * 2 + who[2]], sb.at[h, me], p_send.at[h, d], p_recv.at[h, d], who)
            for d, who in enumerate(peers)
        ]

    def regroup(h):
        for c in reduce_copies(h):
            c.wait()
        mine = acc[h, :, b]
        for d in range(nb - 1):
            mine = mine + rb[h, d]
        mine = mine.reshape(2 * vv, rows)
        parts = jnp.concatenate(split(mine, 3), axis=0)
        n = 2 * vv
        moved = dot(parts, st[...], NT)
        moved = moved[:n] + moved[n : 2 * n] + moved[2 * n :]
        for o in range(ns):
            pk[h, o] = moved[:, o * cap : (o + 1) * cap]
        for c in regroup_copies(h):
            c.start()
        sb[h, me] = pk[h, me]

    def finish(h):
        for d, c in enumerate(regroup_copies(h)):
            c.wait_send()
            src = lax.rem(me + ns - 1 - d, ns)
            remote(pk.at[h, src], sb.at[h, src], p_send.at[h, d], p_recv.at[h, d], peers[d]).wait_recv()
        got = jnp.concatenate([sb[h, s] for s in range(ns)], axis=1)
        high, low = split(got, 2)
        n = 2 * vv
        both = dot(jnp.concatenate([high, low], axis=0), gh[...], NN)
        loads = both[:n] + both[n:] + dot(high, gl[...], NN)
        out_ref[0, :, h * vv : (h + 1) * vv, :] = loads.reshape(2, vv, loads.shape[1])

    def absorb(h, k):
        for zs, cond in near(k):

            def body(zs=zs):
                slot = zs * 2 + 1 - y
                if k == 1:
                    pl.when(zs == pair)(lambda: arrived_pair(h))
                    pl.when(zs != pair)(lambda: arrived(h, slot))
                else:
                    arrived(h, slot)
                    if k == 0:
                        extra(h).start()
                if h == 0:
                    a_copy(slot).wait()
                multiply(h, slot, xb[h, slot])

            guarded(cond, body)

    for h in range(HALVES):
        if h == 0:
            a_copy(me).wait()
        multiply(h, me, x_ref[h], first=True)
        for k in range(1, nz):
            for side, (zs, cond) in enumerate(near(k)):

                def body(zs=zs, side=side):
                    slot = zs * 2 + y
                    arrived(h, slot)
                    if side == 0:
                        pl.when(z < nz - 1)(lambda: up(h, zs).start())
                    else:
                        pl.when(z > 0)(lambda: down(h, zs).start())
                    if k == 1:
                        pl.when(zs == pair)(lambda: across_part(h).start())
                        pl.when(zs != pair)(lambda: across(h, zs).start())
                    else:
                        across(h, zs).start()

                guarded(cond, body)
            if k == nz - 1 and h + 1 < HALVES:
                start_own(h + 1)
            if k == 1:
                absorb(h, 0)
            for zs, cond in near(k):

                def body(zs=zs):
                    slot = zs * 2 + y
                    if h == 0:
                        a_copy(slot).wait()
                    multiply(h, slot, xb[h, slot])

                guarded(cond, body)
            if k == 1 and h == 0:
                prepare()
            if k == 1 and h > 0:
                regroup(h - 1)
            if k > 1:
                absorb(h, k - 1)
        absorb(h, nz - 1)
        for c in reduce_copies(h):
            c.start()
        if h > 0:
            finish(h - 1)
    regroup(HALVES - 1)
    for h in range(HALVES):
        extra(h).wait_send()
        for k in range(nz):
            for side, (zs, cond) in enumerate(near(k)):

                def body(zs=zs, side=side):
                    if side == 0:
                        pl.when(z < nz - 1)(lambda: up(h, zs).wait_send())
                    if side == 1 or k == 0:
                        pl.when(z > 0)(lambda: down(h, zs).wait_send())
                    if k == 1:
                        pl.when(zs == pair)(lambda: across_part(h).wait_send())
                        pl.when(zs != pair)(lambda: across(h, zs).wait_send())
                    else:
                        across(h, zs).wait_send()

                guarded(cond, body)
    finish(HALVES - 1)


def shards(bem_matrix, surface_field, owner, wet_offset, wet_count, coupling):
    _, rows, cols = bem_matrix.shape
    depth, _, vectors = surface_field.shape
    nz = lax.axis_size("sub")
    nb = lax.axis_size("blk")
    ns = 2 * nz
    vv = vectors // (nb * HALVES)
    cap = max(2 * rows // ns, 128)
    wide = 2 * nb * vv
    wet, loads = coupling.shape[1:]
    packed = surface_field.reshape(depth, 2, nb, HALVES, vv).transpose(3, 1, 2, 4, 0)
    packed = packed.reshape(HALVES, wide, depth)
    vmem = pl.BlockSpec(memory_space=pltpu.VMEM)
    smem = pl.BlockSpec(memory_space=pltpu.SMEM)
    dma = pltpu.SemaphoreType.DMA
    return pl.pallas_call(
        functools.partial(kernel, (nz, nb, vv, depth, cap)),
        out_shape=jax.ShapeDtypeStruct((1, 2, HALVES * vv, loads), F32),
        in_specs=[pl.BlockSpec(memory_space=pl.ANY), vmem, vmem, smem, smem, vmem],
        out_specs=vmem,
        scratch_shapes=[
            pltpu.VMEM((ns, 2, rows, depth), BF),
            pltpu.VMEM((HALVES, ns, wide, depth), BF),
            pltpu.VMEM((HALVES, 2, nb, vv, rows), F32),
            pltpu.VMEM((HALVES, nb - 1, 2, vv, rows), F32),
            pltpu.VMEM((ns, ns, 128), F32),
            pltpu.VMEM((ns * cap, rows), BF),
            pltpu.VMEM((ns * cap, loads), BF),
            pltpu.VMEM((ns * cap, loads), BF),
            pltpu.VMEM((HALVES, ns, 2 * vv, cap), F32),
            pltpu.VMEM((HALVES, ns, 2 * vv, cap), F32),
            dma((ns,)),
            dma((HALVES, ns)),
            dma((HALVES,)),
            dma((HALVES, nz)),
            dma((HALVES, nz)),
            dma((HALVES, nz)),
            dma((HALVES,)),
            dma((HALVES, nb - 1)),
            dma((HALVES, nb - 1)),
            dma((ns - 1,)),
            dma((ns - 1,)),
            dma((HALVES, ns - 1)),
            dma((HALVES, ns - 1)),
        ],
        compiler_params=pltpu.CompilerParams(
            collective_id=0, has_side_effects=True, vmem_limit_bytes=60 * 2**20
        ),
    )(bem_matrix, packed, owner.reshape(1, rows), wet_offset, wet_count, coupling)


def solution(mesh):
    return jax.shard_map(
        shards,
        mesh=mesh,
        in_specs=(
            P(None, ("sub", "rows"), "blk"),
            P(("blk", "sub", "rows"), None, None),
            P(("sub", "rows")),
            P(),
            P(),
            P(("sub", "rows"), None, None),
        ),
        out_specs=P(("sub", "rows"), None, "blk", None),
        check_vma=False,
    )
```

time: 178 us -> 73.1 us (0.41)
  waiting for transfers between devices: 80.7 us -> 0 us
  Pallas kernels: 0 us -> 69.2 us
  blocking collectives: 24 us -> 0 us
  other arithmetic: 19.2 us -> 0 us
  matrix products: 14.5 us -> 0 us
  between operations: 14.2 us -> 0.02 us
  local copies, waits for them, and re-layouts: 17.3 us -> 3.71 us
  starting transfers between devices: 6.97 us -> 0 us
    all_gather x1 -> x0, waiting for transfers between devices: 74.7 us -> none  [shards(): piece = lax.all_gather(surface_field, ('sub', 'rows'), axis=0, tiled=True)]
    pallas_call x0 -> x1, Pallas kernels: none -> 69.2 us  [shards(): pl.pallas_call(functools.partial(kernel, (nz, nb, vv, depth, cap)), out_s...]
    unnamed x1 -> x0, blocking collectives: 24 us -> none
    add x2 -> x0, other arithmetic: 15.6 us -> none  [the longest x1 14.9 us: shards(): slot_value + 1.0]
    dot_general x5 -> x0, matrix products: 14.5 us -> none  [the longest x1 9.35 us: shards(): products = jnp.dot(stacked, flat_piece, preferred_element_type=jnp.float32)]
    reshape x2 -> x0, local copies, waits for them, and re-layouts: 11.6 us -> none  [the longest x1 11.2 us: shards(): flat_piece = piece.reshape(piece.shape[0], 2 * vectors)]
    all_to_all x2 -> x0, starting transfers between devices: 6.93 us -> none  [the longest x1 3.56 us: shards(): lax.all_to_all(sent_values, ('sub', 'rows'), split_axis=0, concat_axis=0,...]
    unnamed x3 -> x0, waiting for transfers between devices: 3.93 us -> none
  transfers between devices with their start and end apart: 4 -> 0, of which waited for: 3 -> 0; matrix products, arithmetic and copies ran while one was open for 14% -> 0% of each run, Pallas kernels for 0% -> 0%
where the time goes in v1:
time: 73.1 us; the launch traced here: 73 us
  Pallas kernels  69.2 us (95%)
  local copies, waits for them, and re-layouts  3.71 us (5%)
    pallas_call x1, Pallas kernels, shards(): pl.pallas_call(functools.partial(kernel, (nz, nb, vv, depth, cap)), out_s...  69.2 us
    unnamed x2, local copies, waits for them, and re-layouts  2.87 us

profile of v1, /device:TPU:0, one launch (start us, length us, event | category | flops | bytes accessed | tf_op | source)
XLA Modules:
  0.0 73.0 jit_solution(16297758547208309436)
XLA Ops:
  0.0 1.3 %copy.8 = bf16[1024,2,128]{0,2,1:T(8,128)(2,1)S(1)} copy(bf16[1024,2,128]{2,1,0:T(2,128)(2,1)} %param.7) | data formatting | bytes 1048576 | tf_op args[1]
  1.3 0.8 %copy.9 = bf16[2,2,4,16,1024]{4,3,2,1,0:T(8,128)(2,1)} copy(bf16[2,2,4,16,1024]{4,3,0,2,1:T(8,128)(2,1)S(1)} %bitcast.6) | data formatting | bytes 1048576 | tf_op jit(solution)/shard_map/transpose | solution.py:319
  2.2 69.2 %shard_map.64 = f32[1,2,32,512]{3,2,1,0:T(8,128)} custom-call(bf16[2,512,8192]{2,1,0:T(8,128)(2,1)} %a_ref.1, bf16[2,128,1024]{2,1,0:T(8,128)(2,1)} %bitcast.5, s32[1,512]{1,0:T(1,128)} %bitcast.7, s32[8]{0:T(128)} %off_ref.1, s32[8]{0:T(128)} %cnt_ref.1, f32[1,512,512]{2,1,0:T(8,128)} %coup_ref.1), custom_call_target="tpu_custom_call" | custom-call | tf_op jit(solution)/shard_map/pallas_call | solution.py:324
  71.4 1.6 %copy.11 = f32[1,2,32,512]{3,2,1,0:T(8,128)} copy(f32[1,2,32,512]{3,2,1,0:T(8,128)} %shard_map.64) | data formatting | bytes 262144
